TPU v7x, 32 devices: a whole 2x2x4 slice. The times are simulated.
32 devices in a mesh: groups: 2 (over y), dp: 4 (over z), tensor: 4 (over x, core).
Axes of the slice: x: 2, y: 2, z: 4, core: 2. Of those that a mesh axis runs over, the one named last changes fastest.
Arguments:
- entered_tokens: bfloat16 [1024, 8192], P(('groups', 'dp'), 'tensor'), parts along dimension 0, may hold values from -6 to 6
- output_grad: bfloat16 [1024, 1024], P(('groups', 'dp'), 'tensor'), parts along dimension 0, may hold values from -6 to 6
- value_matrix: bfloat16 [8192, 1024], P(None, 'tensor'), may hold values from -0.0625 to 0.0625
- adapter_down: bfloat16 [16, 16, 8192], P(('groups', 'dp'), None, 'tensor'), parts along dimension 0, may hold values from -0.0625 to 0.0625
- adapter_up: bfloat16 [16, 16, 1024], P(('groups', 'dp'), None, 'tensor'), parts along dimension 0, may hold values from -1.5 to 1.5
- segment_owner_adapter: int32 [8], P('groups'), parts along dimension 0, may hold values from 0 to 7, as said below
- adapter_storage: int32 [16], P('groups'), parts along dimension 0, may hold values from 0 to 7, as said below
Outputs:
- layer_input_grad: bfloat16 [1024, 8192], P(('groups', 'dp'), 'tensor'), parts along dimension 0
- grad_down: float32 [16, 16, 8192], P(('groups', 'dp'), None, 'tensor'), parts along dimension 0
- grad_up: float32 [16, 16, 1024], P(('groups', 'dp'), None, 'tensor'), parts along dimension 0
There are 2 independent parts, one for each index of `groups`. A program takes and returns all parts, laid end to end along the dimension named above; an argument that names none is the same for every part. Nothing has to cross between parts.
Inputs may be any that keep to these rules, and one draw needn't show every extreme that they name: `segment_owner_adapter`: adapter ids of segments; every index of dp stores the adapter of at least one segment. `adapter_storage`: A permutation: each slot holds exactly one adapter.
All inputs are finite; a program needn't handle non-finite values.
Results may differ from a plain program's by a relative error of at most 0.001.
Values may be sent and summed in bfloat16 or wider, within the bound.
A program may use at most 64 MiB of HBM per device.

v0:
```python
import jax
import jax.numpy as jnp
from jax import lax
from jax.sharding import PartitionSpec as P

SEGMENT_TOKENS = 128


adapter_scale = 2.0
exact_check = lax.Precision.HIGHEST


def on_device(
    entered_tokens,
    output_grad,
    value_matrix,
    adapter_down,
    adapter_up,
    segment_owner_adapter,
    adapter_storage,
):
    token_rows, feature_columns = entered_tokens.shape
    per_holder = adapter_down.shape[0]
    rank_width = adapter_down.shape[1]
    adapter_count = adapter_storage.shape[0]
    dp_count = lax.axis_size("dp")
    my_index = lax.axis_index("dp")
    segment_count = token_rows // SEGMENT_TOKENS
    slots_all = jnp.take(adapter_storage, segment_owner_adapter)
    my_slots = lax.dynamic_slice_in_dim(slots_all, my_index * segment_count, segment_count)
    my_adapters = lax.dynamic_slice_in_dim(
        segment_owner_adapter, my_index * segment_count, segment_count
    )
    all_down, all_up = (
        lax.all_gather(adapter_down, "dp", axis=0, tiled=True),
        lax.all_gather(adapter_up, "dp", axis=0, tiled=True),
    )
    picked_down = jnp.take(all_down, my_slots, axis=0)
    picked_up = jnp.take(all_up, my_slots, axis=0)
    kv_cols = output_grad.shape[1]
    seg_input = entered_tokens.reshape(segment_count, SEGMENT_TOKENS, feature_columns)
    seg_grad = output_grad.reshape(segment_count, SEGMENT_TOKENS, kv_cols)
    in_part = jnp.einsum("std,srd->str", seg_input, picked_down, preferred_element_type=jnp.float32)
    grad_part = jnp.einsum("stk,srk->str", seg_grad, picked_up, preferred_element_type=jnp.float32)
    low_in, rank_space_grad = lax.psum((in_part, grad_part), "tensor")
    weight_mine = lax.all_to_all(value_matrix, "tensor", split_axis=0, concat_axis=1, tiled=True)
    grad_whole = lax.all_gather(output_grad, "tensor", axis=1, tiled=True)
    frozen_sum = jnp.einsum(
        "tk,dk->td", grad_whole, weight_mine, preferred_element_type=jnp.float32
    )
    adapter_term = adapter_scale * jnp.einsum(
        "mgu,mue->mge", rank_space_grad, picked_down.astype(jnp.float32), precision=exact_check
    )
    layer_input_grad = (frozen_sum + adapter_term.reshape(token_rows, feature_columns)).astype(
        jnp.bfloat16
    )
    adapter_hits = (
        segment_owner_adapter[:, None] == jnp.arange(adapter_count, dtype=jnp.int32)[None, :]
    )
    segment_counts = SEGMENT_TOKENS * jnp.sum(adapter_hits.astype(jnp.int32), axis=0)
    local_counts = jnp.take(segment_counts, my_adapters)
    segment_factor = adapter_scale / jnp.maximum(local_counts, SEGMENT_TOKENS).astype(jnp.float32)
    down_terms = (
        jnp.einsum(
            "str,std->srd", rank_space_grad, seg_input.astype(jnp.float32), precision=exact_check
        )
        * segment_factor[:, None, None]
    )
    up_terms = (
        jnp.einsum("str,stk->srk", low_in, seg_grad.astype(jnp.float32), precision=exact_check)
        * segment_factor[:, None, None]
    )
    choose_slot = (my_slots[:, None] == jnp.arange(adapter_count, dtype=jnp.int32)[None, :]).astype(
        jnp.float32
    )
    send_down = jnp.einsum("sa,srd->ard", choose_slot, down_terms, precision=exact_check)
    send_up = jnp.einsum("sa,srk->ark", choose_slot, up_terms, precision=exact_check)
    recv_down, recv_up = (
        lax.all_to_all(send_down, "dp", split_axis=0, concat_axis=0, tiled=True),
        lax.all_to_all(send_up, "dp", split_axis=0, concat_axis=0, tiled=True),
    )
    grad_down = jnp.sum(
        recv_down.reshape(dp_count, per_holder, rank_width, feature_columns), axis=0
    )
    grad_up = jnp.sum(recv_up.reshape(dp_count, per_holder, rank_width, kv_cols), axis=0)
    return (layer_input_grad, grad_down, grad_up)


def solution(mesh):
    in_specs = (
        P(("groups", "dp"), "tensor"),
        P(("groups", "dp"), "tensor"),
        P(None, "tensor"),
        P(("groups", "dp"), None, "tensor"),
        P(("groups", "dp"), None, "tensor"),
        P("groups"),
        P("groups"),
    )
    out_specs = (
        P(("groups", "dp"), "tensor"),
        P(("groups", "dp"), None, "tensor"),
        P(("groups", "dp"), None, "tensor"),
    )
    return jax.shard_map(
        on_device, mesh=mesh, in_specs=in_specs, out_specs=out_specs, check_vma=False
    )
```

profile of v0, /device:TPU:0, one launch (start us, length us, event | category | flops | bytes accessed | tf_op | source)
XLA Modules:
  0.0 160.0 jit_solution(16005245703577292686)
XLA Ops:
  0.6 0.7 compare_select_fusion
  1.4 0.7 convert_reduce_fusion
  2.1 1.2 dynamic_slice.7
  4.7 1.3 gather_fusion
  6.0 0.7 and_select_fusion
  6.6 0.6 dynamic_slice.6
  9.8 0.7 dynamic-slice.10
  11.2 0.7 compare_convert_fusion
  11.8 15.1 %all_gather.10 = bf16[8,16,256]{2,1,0:T(8,128)(2,1)S(1)} all-gather(bf16[2,16,256]{2,1,0:T(8,128)(2,1)} %param.11), channel_id=1, replica_groups=mesh['groups'=2,'dp'=4,'tensor'=4] {'dp'}, dimensions={0}, use_global_device_ids=true | all-gather | bytes 81920 | tf_op jit(solution)/shard_map/all_gather | solution.py:36
  26.9 16.2 %all_gather.11 = bf16[8,16,2048]{2,1,0:T(8,128)(2,1)S(1)} all-gather(bf16[2,16,2048]{2,1,0:T(8,128)(2,1)} %param.10), channel_id=1, replica_groups=mesh['groups'=2,'dp'=4,'tensor'=4] {'dp'}, dimensions={0}, use_global_device_ids=true | all-gather | bytes 655360 | tf_op jit(solution)/shard_map/all_gather | solution.py:35
  43.2 1.0 convolution_bitcast_fusion
  44.4 10.2 %all-reduce = (f32[128,16]{0,1:T(8,128)S(1)}, f32[128,16]{0,1:T(8,128)S(1)}) all-reduce(f32[128,16]{0,1:T(8,128)S(1)} %convolution_bitcast_fusion, f32[128,16]{0,1:T(8,128)S(1)} %convolution_bitcast_fusion.1), channel_id=1, replica_groups=mesh['groups'=2,'dp'=4,'tensor'=4] {'tensor'}, use_global_device_ids=true, to_apply=%region_0.1 | all-reduce | flops 4096 | bytes 32768 | tf_op jit(solution)/shard_map/psum | solution.py:45
  54.6 1.0 convolution_multiply_fusion.2
  55.6 0.8 broadcast_multiply_fusion.1
  56.3 3.7 %all-to-all-start.2 = ((f32[8,16,256]{2,1,0:T(8,128)}), f32[8,16,256]{2,1,0:T(8,128)S(1)}, u32[]{:S(2)}, u32[]{:S(2)}) async-start(f32[8,16,256]{2,1,0:T(8,128)} %broadcast_multiply_fusion.1), calls=%async_computation.2 | async-start | bytes 262144 | tf_op jit(solution)/shard_map/all_to_all | solution.py:80
  60.5 5.4 %all-to-all-done.2 = f32[8,16,256]{2,1,0:T(8,128)S(1)} async-done(((f32[8,16,256]{2,1,0:T(8,128)}), f32[8,16,256]{2,1,0:T(8,128)S(1)}, u32[]{:S(2)}, u32[]{:S(2)}) %all-to-all-start.2) | async-done | bytes 131104 | tf_op jit(solution)/shard_map/all_to_all | solution.py:80
  65.9 26.6 %all_to_all.29 = f32[8,16,2048]{2,1,0:T(8,128)S(1)} all-to-all(f32[8,16,2048]{2,1,0:T(8,128)S(1)} %broadcast_multiply_fusion), channel_id=1, replica_groups=mesh['groups'=2,'dp'=4,'tensor'=4] {'dp'}, dimensions={0} | all-to-all | bytes 2097152 | tf_op jit(solution)/shard_map/all_to_all | solution.py:79
  92.5 5.0 %all-to-all-start = ((bf16[4,2048,256]{2,1,0:T(8,128)(2,1)}), bf16[4,2048,256]{2,1,0:T(8,128)(2,1)}, u32[]{:S(2)}, u32[]{:S(2)}) async-start(bf16[4,2048,256]{2,1,0:T(8,128)(2,1)} %bitcast.32), calls=%async_computation | async-start | bytes 8388608 | tf_op jit(solution)/shard_map/all_to_all | solution.py:46
  97.5 50.4 %all_gather.9 = bf16[128,1024]{1,0:T(8,128)(2,1)S(1)} all-gather(bf16[128,256]{1,0:T(8,128)(2,1)S(1)} %copy-done.1), channel_id=1, replica_groups=mesh['groups'=2,'dp'=4,'tensor'=4] {'tensor'}, dimensions={1}, use_global_device_ids=true | all-gather | bytes 327680 | tf_op jit(solution)/shard_map/all_gather | solution.py:47
  147.9 0.6 convolution_multiply_fusion
  148.5 0.6 reduce_sum.29
  149.2 0.8 reduce_sum.28
  149.9 6.4 %copy.12 = bf16[2048,4,256]{0,2,1:T(8,128)(2,1)} copy(bf16[2048,4,256]{2,0,1:T(8,128)(2,1)} %bitcast.1) | data formatting | bytes 8388608 | tf_op jit(solution)/shard_map/all_to_all | solution.py:46
  156.3 3.7 %fusion = bf16[128,2048]{1,0:T(8,128)(2,1)} fusion(f32[128,2048]{1,0:T(8,128)S(1)} %convolution_multiply_fusion, bf16[128,1024]{1,0:T(8,128)(2,1)S(1)} %all_gather.9, bf16[2048,1024]{0,1:T(8,128)(2,1)} %bitcast.31), kind=kOutput, calls=%fused_computation.3 | convolution fusion | flops 537395200 | bytes 6029312 | tf_op jit(solution)/shard_map/tk,dk->td/dot_general | solution.py:48
  (10 shorter events, 0.8 us)
Async XLA Ops:
  0.6 43.5 %copy-start = (bf16[128,2048]{1,0:T(8,128)(2,1)S(1)}, bf16[128,2048]{1,0:T(8,128)(2,1)}, u32[]{:S(2)}) copy-start(bf16[128,2048]{1,0:T(8,128)(2,1)} %param.7) | copy-start | bytes 1572868
  56.3 9.6 %all-to-all-start.2 = ((f32[8,16,256]{2,1,0:T(8,128)}), f32[8,16,256]{2,1,0:T(8,128)S(1)}, u32[]{:S(2)}, u32[]{:S(2)}) async-start(f32[8,16,256]{2,1,0:T(8,128)} %broadcast_multiply_fusion.1), calls=%async_computation.2 | async-start | bytes 262144 | tf_op jit(solution)/shard_map/all_to_all | solution.py:80
  92.5 5.0 %copy-start.1 = (bf16[128,256]{1,0:T(8,128)(2,1)S(1)}, bf16[128,256]{1,0:T(8,128)(2,1)}, u32[]{:S(2)}) copy-start(bf16[128,256]{1,0:T(8,128)(2,1)} %param.8) | copy-start | bytes 196612
  92.5 57.4 %all-to-all-start = ((bf16[4,2048,256]{2,1,0:T(8,128)(2,1)}), bf16[4,2048,256]{2,1,0:T(8,128)(2,1)}, u32[]{:S(2)}, u32[]{:S(2)}) async-start(bf16[4,2048,256]{2,1,0:T(8,128)(2,1)} %bitcast.32), calls=%async_computation | async-start | bytes 8388608 | tf_op jit(solution)/shard_map/all_to_all | solution.py:46
where the time goes:
time: 161 us; the launch traced here: 160 us
  blocking collectives  118 us (73%)
  local copies, waits for them, and re-layouts  10.2 us (6%)
  starting transfers between devices  8.68 us (5%)
  matrix products  6.83 us (4%)
  waiting for transfers between devices  5.44 us (3%)
  between operations  5.38 us (3%)
  other arithmetic  5.09 us (3%)
    all_gather x1, blocking collectives, on_device(): grad_whole = lax.all_gather(output_grad, 'tensor', axis=1, tiled=True)  50.4 us
    all_to_all x1, blocking collectives, on_device(): lax.all_to_all(send_down, 'dp', split_axis=0, concat_axis=0, tiled=True)  26.6 us
    all_gather x1, blocking collectives, on_device(): lax.all_gather(adapter_down, 'dp', axis=0, tiled=True)  16.2 us
    all_gather x1, blocking collectives, on_device(): lax.all_gather(adapter_up, 'dp', axis=0, tiled=True)  15.1 us
    psum x1, blocking collectives, on_device(): low_in, rank_space_grad = lax.psum((in_part, grad_part), 'tensor')  10.2 us
    all_to_all x1, local copies, waits for them, and re-layouts, on_device(): lax.all_to_all(value_matrix, 'tensor', split_axis=0, concat_axis=1, tiled...  6.4 us
    all_to_all x1, waiting for transfers between devices, on_device(): lax.all_to_all(send_up, 'dp', split_axis=0, concat_axis=0, tiled=True)  5.44 us
    all_to_all x1, starting transfers between devices, on_device(): lax.all_to_all(value_matrix, 'tensor', split_axis=0, concat_axis=1, tiled...  4.99 us
  transfers between devices with their start and end apart: 2, of which 1 were waited for; matrix products, arithmetic and copies ran while one was open for 2% of the time, Pallas kernels for 0%

commit v1 on v0

v1 whole, which is shorter than its diff:
```python
import functools

import jax
import jax.numpy as jnp
from jax import lax
from jax.experimental import pallas as pl
from jax.experimental.pallas import tpu as pltpu
from jax.sharding import PartitionSpec as P

SEGMENT_TOKENS = 128
CORES = 2
adapter_scale = 2.0
EARLY = 2
MESH = pl.DeviceIdType.MESH
F32 = jnp.float32
BF16 = jnp.bfloat16


def dot_last(a, b):
    return lax.dot_general(a, b, (((1,), (1,)), ((), ())), preferred_element_type=F32)


def three_parts(x, axis):
    high = x.astype(BF16)
    rest = x - high.astype(F32)
    mid = rest.astype(BF16)
    low = (rest - mid.astype(F32)).astype(BF16)
    return jnp.concatenate([high, mid, low], axis=axis)


def add_parts(x, rows):
    return x[:rows] + x[rows : 2 * rows] + x[2 * rows :]


def kernel(
    n,
    tn,
    chunk,
    seg_ref,
    store_ref,
    tok_ref,
    grad_ref,
    w_ref,
    down_ref,
    up_ref,
    out_ref,
    gdown_ref,
    gup_ref,
    w_mine,
    w_sib,
    g_sib,
    abuf,
    lbuf,
    tbuf,
    psend,
    prec,
    acc,
    w_sem,
    ws_send,
    ws_recv,
    g_sem,
    a_send,
    a_recv,
    l_send,
    l_recv,
    t_send,
    t_recv,
    p_send,
    p_recv,
):
    per, rank, feat = down_ref.shape
    cols = up_ref.shape[2]
    chips = tn // CORES
    chunks = feat // chunk
    z = lax.axis_index("dp")
    j = lax.axis_index("tensor")
    x = j // CORES
    c = lax.rem(j, CORES)
    sib = x * CORES + (1 - c)

    def w_rows(chip, core, i):
        start = (chip * CORES + core) * feat + i * chunk
        return w_ref.at[pl.ds(pl.multiple_of(start, chunk), chunk)]

    steps = [(s, i) for s in list(range(1, chips)) + [0] for i in range(chunks)]

    w_local = {}
    for s, i in steps:
        chip = lax.rem(x + s, chips)
        w_local[s, i] = pltpu.make_async_copy(
            w_rows(chip, c, i), w_mine.at[s, pl.ds(i * chunk, chunk)], w_sem.at[s, i]
        )
        w_local[s, i].start()

    barrier = pltpu.get_barrier_semaphore()
    for s in range(1, tn):
        pl.semaphore_signal(
            barrier, inc=1, device_id={"tensor": lax.rem(j + s, tn)}, device_id_type=MESH
        )
    for s in range(1, n):
        pl.semaphore_signal(
            barrier, inc=1, device_id={"dp": lax.rem(z + s, n)}, device_id_type=MESH
        )

    my_slot = store_ref[seg_ref[z]]
    my_owner = my_slot // per
    kept = jnp.int32(0)
    user = jnp.int32(0)
    hits = jnp.int32(0)
    for s in range(n):
        slot = store_ref[seg_ref[s]]
        here = slot // per == z
        kept = jnp.where(here, lax.rem(slot, per), kept)
        user = jnp.where(here, s, user)
        hits = hits + jnp.where(seg_ref[s] == seg_ref[z], SEGMENT_TOKENS, 0)
    from_owner = lax.rem(z - my_owner + n, n)
    from_user = lax.rem(z - user + n, n)

    abuf[0, :, :feat] = down_ref[kept]
    abuf[0, :, feat:] = up_ref[kept]

    pl.semaphore_wait(barrier, (tn - 1) + (n - 1))

    a_copies = []
    for s in range(1, n):
        cp = pltpu.make_async_remote_copy(
            src_ref=abuf.at[0],
            dst_ref=abuf.at[s],
            send_sem=a_send.at[s - 1],
            recv_sem=a_recv.at[s - 1],
            device_id={"dp": lax.rem(z + s, n)},
            device_id_type=MESH,
        )
        cp.start()
        a_copies.append(cp)
    g_copy = pltpu.make_async_remote_copy(
        src_ref=grad_ref,
        dst_ref=g_sib,
        send_sem=g_sem.at[0],
        recv_sem=g_sem.at[1],
        device_id={"tensor": sib},
        device_id_type=MESH,
    )
    g_copy.start()
    w_copies = {}
    for s, i in steps:
        chip = lax.rem(x + s, chips)
        cp = pltpu.make_async_remote_copy(
            src_ref=w_rows(chip, 1 - c, i),
            dst_ref=w_sib.at[s, pl.ds(i * chunk, chunk)],
            send_sem=ws_send.at[s, i],
            recv_sem=ws_recv.at[s, i],
            device_id={"tensor": sib},
            device_id_type=MESH,
        )
        cp.start()
        w_copies[s, i] = cp

    def product(s, i):
        w_local[s, i].wait()
        w_copies[s, i].wait_recv()
        rows = pl.ds(i * chunk, chunk)
        return dot_last(grad_ref[...], w_mine[s, rows]) + dot_last(g_sib[...], w_sib[s, rows])

    p_copies = {}

    def send_partial(s, i):
        psend[s - 1, i] = product(s, i)
        cp = pltpu.make_async_remote_copy(
            src_ref=psend.at[s - 1, i],
            dst_ref=prec.at[s - 1, i],
            send_sem=p_send.at[s - 1, i],
            recv_sem=p_recv.at[s - 1, i],
            device_id={"tensor": lax.rem(x + s, chips) * CORES + c},
            device_id_type=MESH,
        )
        cp.start()
        p_copies[s, i] = cp

    partials = [(s, i) for s, i in steps if s > 0]
    g_copy.wait_recv()
    for s, i in partials[:EARLY]:
        send_partial(s, i)

    for cp in a_copies:
        cp.wait_recv()
    lbuf[0, :rank] = dot_last(abuf[from_owner, :, :feat], tok_ref[...])
    lbuf[0, rank:] = dot_last(abuf[from_owner, :, feat:], grad_ref[...])
    l_copies = []
    for s in range(1, tn):
        cp = pltpu.make_async_remote_copy(
            src_ref=lbuf.at[0],
            dst_ref=lbuf.at[s],
            send_sem=l_send.at[s - 1],
            recv_sem=l_recv.at[s - 1],
            device_id={"tensor": lax.rem(j + s, tn)},
            device_id_type=MESH,
        )
        cp.start()
        l_copies.append(cp)
    for s, i in partials[EARLY:]:
        send_partial(s, i)
    for cp in l_copies:
        cp.wait_recv()
    low = lbuf[0]
    for s in range(1, tn):
        low = low + lbuf[s]
    low_in = low[:rank]
    low_grad = low[rank:]

    limit = jnp.maximum(hits, SEGMENT_TOKENS).astype(F32)
    factor = adapter_scale / jnp.full((rank, SEGMENT_TOKENS), limit, F32)
    grad_parts = three_parts(low_grad * factor, 0)
    in_parts = three_parts(low_in * factor, 0)
    tbuf[0, :, :feat] = add_parts(
        jnp.dot(grad_parts, tok_ref[...], preferred_element_type=F32), rank
    )
    tbuf[0, :, feat:] = add_parts(
        jnp.dot(in_parts, grad_ref[...], preferred_element_type=F32), rank
    )
    t_copies = []
    for s in range(1, n):
        cp = pltpu.make_async_remote_copy(
            src_ref=tbuf.at[0],
            dst_ref=tbuf.at[s],
            send_sem=t_send.at[s - 1],
            recv_sem=t_recv.at[s - 1],
            device_id={"dp": lax.rem(z + s, n)},
            device_id_type=MESH,
        )
        cp.start()
        t_copies.append(cp)

    left = three_parts(jnp.transpose(adapter_scale * low_grad), 1)
    for i in range(chunks):
        span = pl.ds(i * chunk, chunk)
        down = abuf[from_owner, :, span]
        acc[i] = product(0, i) + jnp.dot(
            left, jnp.concatenate([down, down, down], axis=0), preferred_element_type=F32
        )
    for i in range(chunks):
        total = acc[i]
        for s in range(1, chips):
            p_copies[s, i].wait_recv()
            total = total + prec[s - 1, i]
        out_ref[:, pl.ds(i * chunk, chunk)] = total.astype(BF16)

    for cp in t_copies:
        cp.wait_recv()
    for k in range(per):
        mine = jnp.where(kept == k, 1.0, 0.0).astype(F32)
        gdown_ref[k] = tbuf[from_user, :, :feat] * mine
        gup_ref[k] = tbuf[from_user, :, feat:] * mine

    g_copy.wait_send()
    for group in (a_copies, l_copies, t_copies, w_copies.values(), p_copies.values()):
        for cp in group:
            cp.wait_send()


def on_device(
    n,
    tn,
    entered_tokens,
    output_grad,
    value_matrix,
    adapter_down,
    adapter_up,
    segment_owner_adapter,
    adapter_storage,
):
    tokens, feat = entered_tokens.shape
    cols = output_grad.shape[1]
    per, rank, _ = adapter_down.shape
    assert tokens == SEGMENT_TOKENS and segment_owner_adapter.shape[0] == n
    chips = tn // CORES
    chunk = min(512, feat)
    chunks = feat // chunk
    vmem = pl.BlockSpec(memory_space=pltpu.VMEM)
    smem = pl.BlockSpec(memory_space=pltpu.SMEM)
    dma = pltpu.SemaphoreType.DMA
    return pl.pallas_call(
        functools.partial(kernel, n, tn, chunk),
        out_shape=(
            jax.ShapeDtypeStruct((tokens, feat), BF16),
            jax.ShapeDtypeStruct((per, rank, feat), F32),
            jax.ShapeDtypeStruct((per, rank, cols), F32),
        ),
        in_specs=[smem, smem, vmem, vmem, pl.BlockSpec(memory_space=pl.ANY), vmem, vmem],
        out_specs=(vmem, vmem, vmem),
        scratch_shapes=[
            pltpu.VMEM((chips, feat, cols), BF16),
            pltpu.VMEM((chips, feat, cols), BF16),
            pltpu.VMEM((tokens, cols), BF16),
            pltpu.VMEM((n, rank, feat + cols), BF16),
            pltpu.VMEM((tn, 2 * rank, tokens), F32),
            pltpu.VMEM((n, rank, feat + cols), F32),
            pltpu.VMEM((chips - 1, chunks, tokens, chunk), F32),
            pltpu.VMEM((chips - 1, chunks, tokens, chunk), F32),
            pltpu.VMEM((chunks, tokens, chunk), F32),
            dma((chips, chunks)),
            dma((chips, chunks)),
            dma((chips, chunks)),
            dma((2,)),
            dma((n - 1,)),
            dma((n - 1,)),
            dma((tn - 1,)),
            dma((tn - 1,)),
            dma((n - 1,)),
            dma((n - 1,)),
            dma((chips - 1, chunks)),
            dma((chips - 1, chunks)),
        ],
        compiler_params=pltpu.CompilerParams(
            collective_id=0, has_side_effects=True, vmem_limit_bytes=40 * 1024 * 1024
        ),
        cost_estimate=pl.CostEstimate(
            flops=2 * tokens * feat * cols * tn, bytes_accessed=2 * value_matrix.size, transcendentals=0
        ),
    )(
        segment_owner_adapter,
        adapter_storage,
        entered_tokens,
        output_grad,
        value_matrix,
        adapter_down,
        adapter_up,
    )


def solution(mesh):
    in_specs = (
        P(("groups", "dp"), "tensor"),
        P(("groups", "dp"), "tensor"),
        P(None, "tensor"),
        P(("groups", "dp"), None, "tensor"),
        P(("groups", "dp"), None, "tensor"),
        P("groups"),
        P("groups"),
    )
    out_specs = (
        P(("groups", "dp"), "tensor"),
        P(("groups", "dp"), None, "tensor"),
        P(("groups", "dp"), None, "tensor"),
    )
    body = functools.partial(on_device, mesh.shape["dp"], mesh.shape["tensor"])
    return jax.shard_map(
        body, mesh=mesh, in_specs=in_specs, out_specs=out_specs, check_vma=False
    )
```

time: 161 us -> 44.9 us (0.28)
  the two profiles are of different devices: /device:TPU:0 before, /device:TPU:9 now
where the time goes in v1:
time: 44.9 us; the launch traced here: 44.5 us
  Pallas kernels  34.8 us (78%)
  local copies, waits for them, and re-layouts  9.1 us (20%)
  between operations  0.66 us (1%)
    pallas_call x1, Pallas kernels, on_device(): pl.pallas_call(functools.partial(kernel, n, tn, chunk), out_shape=(jax.Sh...  34.8 us
    unnamed x17, local copies, waits for them, and re-layouts  9.1 us

profile of v1, /device:TPU:9, one launch (start us, length us, event | category | flops | bytes accessed | tf_op | source)
XLA Modules:
  0.0 44.5 jit_solution(11200212345083225250)
XLA Ops:
  0.6 0.0 copy-start
  0.6 2.2 %copy-done = bf16[8192,256]{1,0:T(8,128)(2,1)S(1)} copy-done((bf16[8192,256]{1,0:T(8,128)(2,1)S(1)}, bf16[8192,256]{1,0:T(8,128)(2,1)}, u32[]{:S(2)}) %copy-start) | copy-done | bytes 4194328
  2.8 0.0 copy-start.1
  2.8 1.0 %copy-done.1 = bf16[128,2048]{1,0:T(8,128)(2,1)S(1)} copy-done((bf16[128,2048]{1,0:T(8,128)(2,1)S(1)}, bf16[128,2048]{1,0:T(8,128)(2,1)}, u32[]{:S(2)}) %copy-start.1) | copy-done | bytes 524312
  3.9 0.0 copy-start.2
  3.9 0.9 %copy-done.2 = bf16[2,16,2048]{2,1,0:T(8,128)(2,1)S(1)} copy-done((bf16[2,16,2048]{2,1,0:T(8,128)(2,1)S(1)}, bf16[2,16,2048]{2,1,0:T(8,128)(2,1)}, u32[]{:S(2)}) %copy-start.2) | copy-done | bytes 131096
  4.8 0.0 copy-start.3
  4.8 0.8 %copy-done.3 = bf16[128,256]{1,0:T(8,128)(2,1)S(1)} copy-done((bf16[128,256]{1,0:T(8,128)(2,1)S(1)}, bf16[128,256]{1,0:T(8,128)(2,1)}, u32[]{:S(2)}) %copy-start.3) | copy-done | bytes 65560
  5.6 0.0 copy-start.4
  5.6 0.7 %copy-done.4 = bf16[2,16,256]{2,1,0:T(8,128)(2,1)S(1)} copy-done((bf16[2,16,256]{2,1,0:T(8,128)(2,1)S(1)}, bf16[2,16,256]{2,1,0:T(8,128)(2,1)}, u32[]{:S(2)}) %copy-start.4) | copy-done | bytes 16408
  6.3 0.0 copy-start.5
  6.3 0.7 %copy-done.5 = s32[4]{0:T(128)S(1)} copy-done((s32[4]{0:T(128)S(1)}, s32[4]{0:T(128)}, u32[]{:S(2)}) %copy-start.5) | copy-done | bytes 40
  7.0 0.0 copy-start.6
  7.0 0.7 %copy-done.6 = s32[8]{0:T(128)S(1)} copy-done((s32[8]{0:T(128)S(1)}, s32[8]{0:T(128)}, u32[]{:S(2)}) %copy-start.6) | copy-done | bytes 56
  7.6 34.8 %shard_map.94 = (bf16[128,2048]{1,0:T(8,128)(2,1)S(1)}, f32[2,16,2048]{2,1,0:T(8,128)S(1)}, f32[2,16,256]{2,1,0:T(8,128)S(1)}) custom-call(s32[4]{0:T(128)S(1)} %copy-done.5, s32[8]{0:T(128)S(1)} %copy-done.6, bf16[128,2048]{1,0:T(8,128)(2,1)S(1)} %copy-done.1, bf16[128,256]{1,0:T(8,128)(2,1)S(1)} %copy-done.3, bf16[8192,256]{1,0:T(8,128)(2,1)S(1)} %copy-done, ...), custom_call_target="tpu_custom_call" | custom-call | flops 536870912 | bytes 4194304 | tf_op jit(solution)/shard_map/pallas_call | solution.py:282
  42.4 0.8 %copy.13 = bf16[128,2048]{1,0:T(8,128)(2,1)} copy(bf16[128,2048]{1,0:T(8,128)(2,1)S(1)} %get-tuple-element.6) | data formatting | bytes 1048576
  43.2 0.7 %copy.14 = f32[2,16,2048]{2,1,0:T(8,128)} copy(f32[2,16,2048]{2,1,0:T(8,128)S(1)} %get-tuple-element.7) | data formatting | bytes 524288
  43.9 0.6 %copy.15 = f32[2,16,256]{2,1,0:T(8,128)} copy(f32[2,16,256]{2,1,0:T(8,128)S(1)} %get-tuple-element.8) | data formatting | bytes 65536
Async XLA Ops:
  0.6 2.2 %copy-start = (bf16[8192,256]{1,0:T(8,128)(2,1)S(1)}, bf16[8192,256]{1,0:T(8,128)(2,1)}, u32[]{:S(2)}) copy-start(bf16[8192,256]{1,0:T(8,128)(2,1)} %w_ref.1) | copy-start | bytes 12582916
  2.8 1.0 %copy-start.1 = (bf16[128,2048]{1,0:T(8,128)(2,1)S(1)}, bf16[128,2048]{1,0:T(8,128)(2,1)}, u32[]{:S(2)}) copy-start(bf16[128,2048]{1,0:T(8,128)(2,1)} %tok_ref.1) | copy-start | bytes 1572868
  3.9 0.9 %copy-start.2 = (bf16[2,16,2048]{2,1,0:T(8,128)(2,1)S(1)}, bf16[2,16,2048]{2,1,0:T(8,128)(2,1)}, u32[]{:S(2)}) copy-start(bf16[2,16,2048]{2,1,0:T(8,128)(2,1)} %down_ref.1) | copy-start | bytes 393220
  4.8 0.8 %copy-start.3 = (bf16[128,256]{1,0:T(8,128)(2,1)S(1)}, bf16[128,256]{1,0:T(8,128)(2,1)}, u32[]{:S(2)}) copy-start(bf16[128,256]{1,0:T(8,128)(2,1)} %grad_ref.1) | copy-start | bytes 196612
  5.6 0.7 %copy-start.4 = (bf16[2,16,256]{2,1,0:T(8,128)(2,1)S(1)}, bf16[2,16,256]{2,1,0:T(8,128)(2,1)}, u32[]{:S(2)}) copy-start(bf16[2,16,256]{2,1,0:T(8,128)(2,1)} %up_ref.1) | copy-start | bytes 49156
  6.3 0.7 %copy-start.5 = (s32[4]{0:T(128)S(1)}, s32[4]{0:T(128)}, u32[]{:S(2)}) copy-start(s32[4]{0:T(128)} %seg_ref.1) | copy-start | bytes 52
  7.0 0.7 %copy-start.6 = (s32[8]{0:T(128)S(1)}, s32[8]{0:T(128)}, u32[]{:S(2)}) copy-start(s32[8]{0:T(128)} %store_ref.1) | copy-start | bytes 100

commit v2 on v1

--- a/solution.py
+++ b/solution.py
@@ -10,6 +10,7 @@
 SEGMENT_TOKENS = 128
 CORES = 2
 adapter_scale = 2.0
+VMEM_LIMIT = 60 * 1024 * 1024
 EARLY = 2
 MESH = pl.DeviceIdType.MESH
 F32 = jnp.float32
@@ -36,16 +37,23 @@
     n,
     tn,
     chunk,
+    seg_hbm,
+    store_hbm,
+    tok_hbm,
+    grad_hbm,
+    w_ref,
+    down_hbm,
+    up_hbm,
+    out_ref,
+    gdown_ref,
+    gup_ref,
     seg_ref,
     store_ref,
     tok_ref,
     grad_ref,
-    w_ref,
     down_ref,
     up_ref,
-    out_ref,
-    gdown_ref,
-    gup_ref,
+    in_sem,
     w_mine,
     w_sib,
     g_sib,
@@ -82,6 +90,22 @@
         start = (chip * CORES + core) * feat + i * chunk
         return w_ref.at[pl.ds(pl.multiple_of(start, chunk), chunk)]
 
+    loads = [
+        pltpu.make_async_copy(src, dst, in_sem.at[k])
+        for k, (src, dst) in enumerate(
+            (
+                (seg_hbm, seg_ref),
+                (store_hbm, store_ref),
+                (down_hbm, down_ref),
+                (up_hbm, up_ref),
+                (grad_hbm, grad_ref),
+                (tok_hbm, tok_ref),
+            )
+        )
+    ]
+    for cp in loads:
+        cp.start()
+
     steps = [(s, i) for s in list(range(1, chips)) + [0] for i in range(chunks)]
 
     w_local = {}
@@ -102,6 +126,8 @@
             barrier, inc=1, device_id={"dp": lax.rem(z + s, n)}, device_id_type=MESH
         )
 
+    for cp in loads[:4]:
+        cp.wait()
     my_slot = store_ref[seg_ref[z]]
     my_owner = my_slot // per
     kept = jnp.int32(0)
@@ -133,6 +159,7 @@
         )
         cp.start()
         a_copies.append(cp)
+    loads[4].wait()
     g_copy = pltpu.make_async_remote_copy(
         src_ref=grad_ref,
         dst_ref=g_sib,
@@ -182,6 +209,7 @@
     for s, i in partials[:EARLY]:
         send_partial(s, i)
 
+    loads[5].wait()
     for cp in a_copies:
         cp.wait_recv()
     lbuf[0, :rank] = dot_last(abuf[from_owner, :, :feat], tok_ref[...])
@@ -277,7 +305,6 @@
     chunk = min(512, feat)
     chunks = feat // chunk
     vmem = pl.BlockSpec(memory_space=pltpu.VMEM)
-    smem = pl.BlockSpec(memory_space=pltpu.SMEM)
     dma = pltpu.SemaphoreType.DMA
     return pl.pallas_call(
         functools.partial(kernel, n, tn, chunk),
@@ -286,9 +313,16 @@
             jax.ShapeDtypeStruct((per, rank, feat), F32),
             jax.ShapeDtypeStruct((per, rank, cols), F32),
         ),
-        in_specs=[smem, smem, vmem, vmem, pl.BlockSpec(memory_space=pl.ANY), vmem, vmem],
+        in_specs=[pl.BlockSpec(memory_space=pl.ANY)] * 7,
         out_specs=(vmem, vmem, vmem),
         scratch_shapes=[
+            pltpu.SMEM(segment_owner_adapter.shape, jnp.int32),
+            pltpu.SMEM(adapter_storage.shape, jnp.int32),
+            pltpu.VMEM(entered_tokens.shape, BF16),
+            pltpu.VMEM(output_grad.shape, BF16),
+            pltpu.VMEM(adapter_down.shape, BF16),
+            pltpu.VMEM(adapter_up.shape, BF16),
+            dma((6,)),
             pltpu.VMEM((chips, feat, cols), BF16),
             pltpu.VMEM((chips, feat, cols), BF16),
             pltpu.VMEM((tokens, cols), BF16),
@@ -312,7 +346,7 @@
             dma((chips - 1, chunks)),
         ],
         compiler_params=pltpu.CompilerParams(
-            collective_id=0, has_side_effects=True, vmem_limit_bytes=40 * 1024 * 1024
+            collective_id=0, has_side_effects=True, vmem_limit_bytes=VMEM_LIMIT
         ),
         cost_estimate=pl.CostEstimate(
             flops=2 * tokens * feat * cols * tn, bytes_accessed=2 * value_matrix.size, transcendentals=0

time: 44.9 us -> 41 us (0.913)
  local copies, waits for them, and re-layouts: 9.1 us -> 4.92 us
    unnamed x17 -> x3, local copies, waits for them, and re-layouts: 9.1 us -> 4.92 us
where the time goes in v2:
time: 41 us; the launch traced here: 40.7 us
  Pallas kernels  35.1 us (86%)
  local copies, waits for them, and re-layouts  4.92 us (12%)
  between operations  0.64 us (2%)
    pallas_call x1, Pallas kernels, on_device(): pl.pallas_call(functools.partial(kernel, n, tn, chunk), out_shape=(jax.Sh...  35.1 us
    unnamed x3, local copies, waits for them, and re-layouts  4.92 us

profile of v2, /device:TPU:9, one launch (start us, length us, event | category | flops | bytes accessed | tf_op | source)
XLA Modules:
  0.0 40.7 jit_solution(16502089405972234531)
XLA Ops:
  0.6 35.1 %shard_map.94 = (bf16[128,2048]{1,0:T(8,128)(2,1)}, f32[2,16,2048]{2,1,0:T(8,128)}, f32[2,16,256]{2,1,0:T(8,128)}) custom-call(s32[4]{0:T(128)} %seg_hbm.1, s32[8]{0:T(128)} %store_hbm.1, bf16[128,2048]{1,0:T(8,128)(2,1)} %tok_hbm.1, bf16[128,256]{1,0:T(8,128)(2,1)} %grad_hbm.1, bf16[8192,256]{1,0:T(8,128)(2,1)} %w_ref.1, bf16[2,16,2048]{2,1,0:T(8,128)(2,1)} %down_hbm.1, ...), custom_call_target="tpu_custom_call" | custom-call | flops 536870912 | bytes 4194304 | tf_op jit(solution)/shard_map/pallas_call | solution.py:309
  35.7 1.9 %copy.13 = bf16[128,2048]{1,0:T(8,128)(2,1)} copy(bf16[128,2048]{1,0:T(8,128)(2,1)} %get-tuple-element.6) | data formatting | bytes 1048576
  37.6 1.7 %copy.14 = f32[2,16,2048]{2,1,0:T(8,128)} copy(f32[2,16,2048]{2,1,0:T(8,128)} %get-tuple-element.7) | data formatting | bytes 524288
  39.3 1.4 %copy.15 = f32[2,16,256]{2,1,0:T(8,128)} copy(f32[2,16,256]{2,1,0:T(8,128)} %get-tuple-element.8) | data formatting | bytes 65536

commit v3 on v2

--- a/solution.py
+++ b/solution.py
@@ -12,6 +12,7 @@
 adapter_scale = 2.0
 VMEM_LIMIT = 60 * 1024 * 1024
 EARLY = 2
+LATE = 2
 MESH = pl.DeviceIdType.MESH
 F32 = jnp.float32
 BF16 = jnp.bfloat16
@@ -57,9 +58,11 @@
     w_mine,
     w_sib,
     g_sib,
-    abuf,
+    dbuf,
+    ubuf,
     lbuf,
-    tbuf,
+    dterm,
+    uterm,
     psend,
     prec,
     acc,
@@ -142,23 +145,38 @@
     from_owner = lax.rem(z - my_owner + n, n)
     from_user = lax.rem(z - user + n, n)
 
-    abuf[0, :, :feat] = down_ref[kept]
-    abuf[0, :, feat:] = up_ref[kept]
+    ubuf[0] = up_ref[kept]
+    dbuf[0] = down_ref[kept]
 
     pl.semaphore_wait(barrier, (tn - 1) + (n - 1))
 
-    a_copies = []
-    for s in range(1, n):
-        cp = pltpu.make_async_remote_copy(
-            src_ref=abuf.at[0],
-            dst_ref=abuf.at[s],
-            send_sem=a_send.at[s - 1],
-            recv_sem=a_recv.at[s - 1],
-            device_id={"dp": lax.rem(z + s, n)},
-            device_id_type=MESH,
-        )
-        cp.start()
-        a_copies.append(cp)
+    def to_all(axis, count, buf, send_sem, recv_sem):
+        me = lax.axis_index(axis)
+        copies = []
+        for s in range(1, count):
+            cp = pltpu.make_async_remote_copy(
+                src_ref=buf.at[0],
+                dst_ref=buf.at[s],
+                send_sem=send_sem.at[s - 1],
+                recv_sem=recv_sem.at[s - 1],
+                device_id={axis: lax.rem(me + s, count)},
+                device_id_type=MESH,
+            )
+            cp.start()
+            copies.append(cp)
+        return copies
+
+    def arrive(copies):
+        for cp in copies:
+            cp.wait_recv()
+
+    def total_of(buf, count):
+        total = buf[0]
+        for s in range(1, count):
+            total = total + buf[s]
+        return total
+
+    up_copies = to_all("dp", n, ubuf, a_send.at[0], a_recv.at[0])
     loads[4].wait()
     g_copy = pltpu.make_async_remote_copy(
         src_ref=grad_ref,
@@ -182,6 +200,7 @@
         )
         cp.start()
         w_copies[s, i] = cp
+    down_copies = to_all("dp", n, dbuf, a_send.at[1], a_recv.at[1])
 
     def product(s, i):
         w_local[s, i].wait()
@@ -205,64 +224,45 @@
         p_copies[s, i] = cp
 
     partials = [(s, i) for s, i in steps if s > 0]
+    limit = jnp.maximum(hits, SEGMENT_TOKENS).astype(F32)
+    factor = adapter_scale / jnp.full((rank, SEGMENT_TOKENS), limit, F32)
+
+    arrive(up_copies)
+    lbuf[0, 0] = dot_last(ubuf[from_owner], grad_ref[...])
+    lg_copies = to_all("tensor", tn, lbuf.at[0], l_send.at[0], l_recv.at[0])
     g_copy.wait_recv()
     for s, i in partials[:EARLY]:
         send_partial(s, i)
-
     loads[5].wait()
-    for cp in a_copies:
-        cp.wait_recv()
-    lbuf[0, :rank] = dot_last(abuf[from_owner, :, :feat], tok_ref[...])
-    lbuf[0, rank:] = dot_last(abuf[from_owner, :, feat:], grad_ref[...])
-    l_copies = []
-    for s in range(1, tn):
-        cp = pltpu.make_async_remote_copy(
-            src_ref=lbuf.at[0],
-            dst_ref=lbuf.at[s],
-            send_sem=l_send.at[s - 1],
-            recv_sem=l_recv.at[s - 1],
-            device_id={"tensor": lax.rem(j + s, tn)},
-            device_id_type=MESH,
-        )
-        cp.start()
-        l_copies.append(cp)
-    for s, i in partials[EARLY:]:
+    arrive(lg_copies)
+    low_grad = total_of(lbuf.at[0], tn)
+    dterm[0] = add_parts(
+        jnp.dot(three_parts(low_grad * factor, 0), tok_ref[...], preferred_element_type=F32), rank
+    )
+    dt_copies = to_all("dp", n, dterm, t_send.at[0], t_recv.at[0])
+    for s, i in partials[EARLY:LATE]:
         send_partial(s, i)
-    for cp in l_copies:
-        cp.wait_recv()
-    low = lbuf[0]
-    for s in range(1, tn):
-        low = low + lbuf[s]
-    low_in = low[:rank]
-    low_grad = low[rank:]
-
-    limit = jnp.maximum(hits, SEGMENT_TOKENS).astype(F32)
-    factor = adapter_scale / jnp.full((rank, SEGMENT_TOKENS), limit, F32)
-    grad_parts = three_parts(low_grad * factor, 0)
-    in_parts = three_parts(low_in * factor, 0)
-    tbuf[0, :, :feat] = add_parts(
-        jnp.dot(grad_parts, tok_ref[...], preferred_element_type=F32), rank
-    )
-    tbuf[0, :, feat:] = add_parts(
-        jnp.dot(in_parts, grad_ref[...], preferred_element_type=F32), rank
-    )
-    t_copies = []
-    for s in range(1, n):
-        cp = pltpu.make_async_remote_copy(
-            src_ref=tbuf.at[0],
-            dst_ref=tbuf.at[s],
-            send_sem=t_send.at[s - 1],
-            recv_sem=t_recv.at[s - 1],
-            device_id={"dp": lax.rem(z + s, n)},
-            device_id_type=MESH,
-        )
-        cp.start()
-        t_copies.append(cp)
+
+    arrive(down_copies)
+    lbuf[1, 0] = dot_last(dbuf[from_owner], tok_ref[...])
+    li_copies = to_all("tensor", tn, lbuf.at[1], l_send.at[1], l_recv.at[1])
+    for s, i in partials[LATE:]:
+        send_partial(s, i)
+    arrive(li_copies)
+    uterm[0] = add_parts(
+        jnp.dot(
+            three_parts(total_of(lbuf.at[1], tn) * factor, 0),
+            grad_ref[...],
+            preferred_element_type=F32,
+        ),
+        rank,
+    )
+    ut_copies = to_all("dp", n, uterm, t_send.at[1], t_recv.at[1])
 
     left = three_parts(jnp.transpose(adapter_scale * low_grad), 1)
     for i in range(chunks):
         span = pl.ds(i * chunk, chunk)
-        down = abuf[from_owner, :, span]
+        down = dbuf[from_owner, :, span]
         acc[i] = product(0, i) + jnp.dot(
             left, jnp.concatenate([down, down, down], axis=0), preferred_element_type=F32
         )
@@ -273,17 +273,39 @@
             total = total + prec[s - 1, i]
         out_ref[:, pl.ds(i * chunk, chunk)] = total.astype(BF16)
 
-    for cp in t_copies:
-        cp.wait_recv()
+    arrive(dt_copies)
+    arrive(ut_copies)
     for k in range(per):
         mine = jnp.where(kept == k, 1.0, 0.0).astype(F32)
-        gdown_ref[k] = tbuf[from_user, :, :feat] * mine
-        gup_ref[k] = tbuf[from_user, :, feat:] * mine
+        gdown_ref[k] = dterm[from_user] * mine
+        gup_ref[k] = uterm[from_user] * mine
 
     g_copy.wait_send()
-    for group in (a_copies, l_copies, t_copies, w_copies.values(), p_copies.values()):
+    for group in (
+        up_copies,
+        down_copies,
+        lg_copies,
+        li_copies,
+        dt_copies,
+        ut_copies,
+        w_copies.values(),
+        p_copies.values(),
+    ):
         for cp in group:
             cp.wait_send()
+
+
+def write_out(a, b, c, a_out, b_out, c_out, a_held, b_held, c_held, sem):
+    rows = ((a, a_held, a_out), (b, b_held, b_out), (c, c_held, c_out))
+    loads = [pltpu.make_async_copy(r[0], r[1], sem.at[0, k]) for k, r in enumerate(rows)]
+    stores = [pltpu.make_async_copy(r[1], r[2], sem.at[1, k]) for k, r in enumerate(rows)]
+    for cp in loads:
+        cp.start()
+    for load, store in zip(loads, stores):
+        load.wait()
+        store.start()
+    for cp in stores:
+        cp.wait()
 
 
 def on_device(
@@ -306,14 +328,14 @@
     chunks = feat // chunk
     vmem = pl.BlockSpec(memory_space=pltpu.VMEM)
     dma = pltpu.SemaphoreType.DMA
-    return pl.pallas_call(
+    results = pl.pallas_call(
         functools.partial(kernel, n, tn, chunk),
         out_shape=(
             jax.ShapeDtypeStruct((tokens, feat), BF16),
             jax.ShapeDtypeStruct((per, rank, feat), F32),
             jax.ShapeDtypeStruct((per, rank, cols), F32),
         ),
-        in_specs=[pl.BlockSpec(memory_space=pl.ANY)] * 7,
+        in_specs=[pl.BlockSpec(memory_space=pltpu.HBM)] * 7,
         out_specs=(vmem, vmem, vmem),
         scratch_shapes=[
             pltpu.SMEM(segment_owner_adapter.shape, jnp.int32),
@@ -326,9 +348,11 @@
             pltpu.VMEM((chips, feat, cols), BF16),
             pltpu.VMEM((chips, feat, cols), BF16),
             pltpu.VMEM((tokens, cols), BF16),
-            pltpu.VMEM((n, rank, feat + cols), BF16),
-            pltpu.VMEM((tn, 2 * rank, tokens), F32),
-            pltpu.VMEM((n, rank, feat + cols), F32),
+            pltpu.VMEM((n, rank, feat), BF16),
+            pltpu.VMEM((n, rank, cols), BF16),
+            pltpu.VMEM((2, tn, rank, tokens), F32),
+            pltpu.VMEM((n, rank, feat), F32),
+            pltpu.VMEM((n, rank, cols), F32),
             pltpu.VMEM((chips - 1, chunks, tokens, chunk), F32),
             pltpu.VMEM((chips - 1, chunks, tokens, chunk), F32),
             pltpu.VMEM((chunks, tokens, chunk), F32),
@@ -336,12 +360,12 @@
             dma((chips, chunks)),
             dma((chips, chunks)),
             dma((2,)),
-            dma((n - 1,)),
-            dma((n - 1,)),
-            dma((tn - 1,)),
-            dma((tn - 1,)),
-            dma((n - 1,)),
-            dma((n - 1,)),
+            dma((2, n - 1)),
+            dma((2, n - 1)),
+            dma((2, tn - 1)),
+            dma((2, tn - 1)),
+            dma((2, n - 1)),
+            dma((2, n - 1)),
             dma((chips - 1, chunks)),
             dma((chips - 1, chunks)),
         ],
@@ -360,6 +384,14 @@
         adapter_down,
         adapter_up,
     )
+    return pl.pallas_call(
+        write_out,
+        out_shape=tuple(jax.ShapeDtypeStruct(r.shape, r.dtype) for r in results),
+        in_specs=[pl.BlockSpec(memory_space=pl.ANY)] * 3,
+        out_specs=(pl.BlockSpec(memory_space=pl.ANY),) * 3,
+        scratch_shapes=[pltpu.VMEM(r.shape, r.dtype) for r in results] + [dma((2, 3))],
+        compiler_params=pltpu.CompilerParams(vmem_limit_bytes=VMEM_LIMIT),
+    )(*results)
 
 
 def solution(mesh):

time: 41 us -> 37.2 us (0.907)
  the two profiles are of different devices: /device:TPU:9 before, /device:TPU:0 now
where the time goes in v3:
time: 37.2 us; the launch traced here: 37.1 us
  Pallas kernels  36.4 us (98%)
  between operations  0.64 us (2%)
    pallas_call x1, Pallas kernels, on_device(): pl.pallas_call(functools.partial(kernel, n, tn, chunk), out_shape=(jax.Sh...  34.5 us
    pallas_call x1, Pallas kernels, on_device(): pl.pallas_call(write_out, out_shape=tuple((jax.ShapeDtypeStruct(r.shape,...  1.97 us

profile of v3, /device:TPU:0, one launch (start us, length us, event | category | flops | bytes accessed | tf_op | source)
XLA Modules:
  0.0 37.1 jit_solution(9551508977926448238)
XLA Ops:
  0.6 34.5 %shard_map.94 = (bf16[128,2048]{1,0:T(8,128)(2,1)}, f32[2,16,2048]{2,1,0:T(8,128)}, f32[2,16,256]{2,1,0:T(8,128)}) custom-call(s32[4]{0:T(128)} %seg_hbm.1, s32[8]{0:T(128)} %store_hbm.1, bf16[128,2048]{1,0:T(8,128)(2,1)} %tok_hbm.1, bf16[128,256]{1,0:T(8,128)(2,1)} %grad_hbm.1, bf16[8192,256]{1,0:T(8,128)(2,1)} %w_ref.1, bf16[2,16,2048]{2,1,0:T(8,128)(2,1)} %down_hbm.1, ...), custom_call_target="tpu_custom_call" | custom-call | flops 536870912 | bytes 4194304 | tf_op jit(solution)/shard_map/pallas_call | solution.py:331
  35.1 2.0 %shard_map.95 = (bf16[128,2048]{1,0:T(8,128)(2,1)}, f32[2,16,2048]{2,1,0:T(8,128)}, f32[2,16,256]{2,1,0:T(8,128)}) custom-call(bf16[128,2048]{1,0:T(8,128)(2,1)} %get-tuple-element.6.a, f32[2,16,2048]{2,1,0:T(8,128)} %get-tuple-element.7.b, f32[2,16,256]{2,1,0:T(8,128)} %get-tuple-element.8.c), custom_call_target="tpu_custom_call" | custom-call | tf_op jit(solution)/shard_map/pallas_call | solution.py:387

commit v4 on v3

--- a/solution.py
+++ b/solution.py
@@ -11,8 +11,10 @@
 CORES = 2
 adapter_scale = 2.0
 VMEM_LIMIT = 60 * 1024 * 1024
-EARLY = 2
-LATE = 2
+HALVES = 2
+SHARED = 2
+EARLY = 0
+LATE = 1
 MESH = pl.DeviceIdType.MESH
 F32 = jnp.float32
 BF16 = jnp.bfloat16
@@ -38,6 +40,7 @@
     n,
     tn,
     chunk,
+    shared,
     seg_hbm,
     store_hbm,
     tok_hbm,
@@ -59,10 +62,14 @@
     w_sib,
     g_sib,
     dbuf,
+    dstage,
     ubuf,
     lbuf,
     dterm,
+    tstage,
     uterm,
+    wx,
+    gx,
     psend,
     prec,
     acc,
@@ -78,6 +85,11 @@
     t_recv,
     p_send,
     p_recv,
+    d_sem,
+    dt_sem,
+    x_sem,
+    hop_sem,
+    gx_sem,
 ):
     per, rank, feat = down_ref.shape
     cols = up_ref.shape[2]
@@ -88,6 +100,10 @@
     x = j // CORES
     c = lax.rem(j, CORES)
     sib = x * CORES + (1 - c)
+    y = lax.axis_index("groups")
+    z_near = z + 1 - 2 * lax.rem(z, 2)
+    z_far = lax.rem(z + 2, n)
+    half = feat // HALVES
 
     def w_rows(chip, core, i):
         start = (chip * CORES + core) * feat + i * chunk
@@ -109,7 +125,8 @@
     for cp in loads:
         cp.start()
 
-    steps = [(s, i) for s in list(range(1, chips)) + [0] for i in range(chunks)]
+    steps = [(s, i) for s in range(1, chips) for i in range(shared, chunks)]
+    steps += [(0, i) for i in range(chunks)]
 
     w_local = {}
     for s, i in steps:
@@ -128,6 +145,9 @@
         pl.semaphore_signal(
             barrier, inc=1, device_id={"dp": lax.rem(z + s, n)}, device_id_type=MESH
         )
+
+    if shared:
+        pl.semaphore_signal(barrier, inc=1, device_id={"groups": 1 - y}, device_id_type=MESH)
 
     for cp in loads[:4]:
         cp.wait()
@@ -136,19 +156,70 @@
     kept = jnp.int32(0)
     user = jnp.int32(0)
     hits = jnp.int32(0)
+    near_user = jnp.int32(0)
+    near_owner = store_ref[seg_ref[z_near]] // per
     for s in range(n):
         slot = store_ref[seg_ref[s]]
         here = slot // per == z
         kept = jnp.where(here, lax.rem(slot, per), kept)
         user = jnp.where(here, s, user)
+        near_user = jnp.where(slot // per == z_near, s, near_user)
         hits = hits + jnp.where(seg_ref[s] == seg_ref[z], SEGMENT_TOKENS, 0)
     from_owner = lax.rem(z - my_owner + n, n)
     from_user = lax.rem(z - user + n, n)
 
     ubuf[0] = up_ref[kept]
-    dbuf[0] = down_ref[kept]
-
-    pl.semaphore_wait(barrier, (tn - 1) + (n - 1))
+    own_down = down_ref[kept]
+    for h in range(HALVES):
+        dbuf[h, 0] = own_down[:, h * half : (h + 1) * half]
+
+    pl.semaphore_wait(barrier, (tn - 1) + (n - 1) + (1 if shared else 0))
+
+    def remote(src, dst, send_sem, recv_sem, device_id):
+        cp = pltpu.make_async_remote_copy(
+            src_ref=src,
+            dst_ref=dst,
+            send_sem=send_sem,
+            recv_sem=recv_sem,
+            device_id=device_id,
+            device_id_type=MESH,
+        )
+        cp.start()
+        return cp
+
+    routed = []
+
+    def route_first(buf, sem, h):
+        if n == 4:
+            out = [remote(buf.at[h, 0], buf.at[h, 1], sem.at[0, h, 0], sem.at[1, h, 0], {"dp": z_far})]
+        else:
+            out = [
+                remote(
+                    buf.at[h, 0],
+                    buf.at[h, s],
+                    sem.at[0, h, s - 1],
+                    sem.at[1, h, s - 1],
+                    {"dp": lax.rem(z + s, n)},
+                )
+                for s in range(1, n)
+            ]
+        routed.extend(out)
+        return out
+
+    def route_second(buf, stage, sem, h, first, near_wants):
+        if n != 4:
+            return first
+        arrive(first)
+        stage[h] = jnp.where(near_wants == z_far, buf[h, 1], buf[h, 0])
+        cp = remote(stage.at[h], buf.at[h, 2], sem.at[0, h, 1], sem.at[1, h, 1], {"dp": z_near})
+        routed.append(cp)
+        return [cp]
+
+    def route_pick(buf, h, source):
+        if n == 4:
+            other = jnp.where(source == z_far, buf[h, 1], buf[h, 2])
+            return jnp.where(source == z, buf[h, 0], other)
+        return buf[h, lax.rem(z - source + n, n)]
 
     def to_all(axis, count, buf, send_sem, recv_sem):
         me = lax.axis_index(axis)
@@ -178,6 +249,30 @@
 
     up_copies = to_all("dp", n, ubuf, a_send.at[0], a_recv.at[0])
     loads[4].wait()
+
+    share_copies = []
+    if shared:
+        quarter = shared * chunk // 4
+        mine = y * 2 + lax.rem(z, 2)
+        across = (1 - y) * 2 + lax.rem(z, 2)
+        beside = y * 2 + 1 - lax.rem(z, 2)
+        x_copies = []
+        for r in range(CORES):
+            core = c if r == 0 else 1 - c
+            start = ((1 - x) * CORES + core) * feat + mine * quarter
+            x_copies.append(
+                remote(
+                    w_ref.at[pl.ds(pl.multiple_of(start, quarter), quarter)],
+                    wx.at[r, mine],
+                    x_sem.at[0, r],
+                    x_sem.at[1, r],
+                    {"tensor": (1 - x) * CORES + core},
+                )
+            )
+        gx_copy = remote(
+            grad_ref, gx.at[0], gx_sem.at[0, 0], gx_sem.at[1, 0], {"tensor": (1 - x) * CORES + c}
+        )
+        share_copies += x_copies + [gx_copy]
     g_copy = pltpu.make_async_remote_copy(
         src_ref=grad_ref,
         dst_ref=g_sib,
@@ -187,6 +282,7 @@
         device_id_type=MESH,
     )
     g_copy.start()
+    down_first = [route_first(dbuf, d_sem, h) for h in range(HALVES)]
     w_copies = {}
     for s, i in steps:
         chip = lax.rem(x + s, chips)
@@ -200,8 +296,6 @@
         )
         cp.start()
         w_copies[s, i] = cp
-    down_copies = to_all("dp", n, dbuf, a_send.at[1], a_recv.at[1])
-
     def product(s, i):
         w_local[s, i].wait()
         w_copies[s, i].wait_recv()
@@ -233,21 +327,62 @@
     g_copy.wait_recv()
     for s, i in partials[:EARLY]:
         send_partial(s, i)
+    down_second = [
+        route_second(dbuf, dstage, d_sem, h, down_first[h], near_owner) for h in range(HALVES)
+    ]
+    if shared:
+        z_copies = []
+        y_copies = []
+        for r in range(CORES):
+            x_copies[r].wait_recv()
+            block = wx.at[r, mine]
+            z_copies.append(
+                remote(block, block, hop_sem.at[0, 0, r], hop_sem.at[1, 0, r], {"dp": z_near})
+            )
+            y_copies.append(
+                remote(block, block, hop_sem.at[0, 1, r], hop_sem.at[1, 1, r], {"groups": 1 - y})
+            )
+        gx_copy.wait_recv()
+        gx_other = remote(
+            gx.at[0], gx.at[1], gx_sem.at[0, 1], gx_sem.at[1, 1], {"tensor": sib}
+        )
+        share_copies += z_copies + y_copies + [gx_other]
     loads[5].wait()
     arrive(lg_copies)
     low_grad = total_of(lbuf.at[0], tn)
-    dterm[0] = add_parts(
-        jnp.dot(three_parts(low_grad * factor, 0), tok_ref[...], preferred_element_type=F32), rank
-    )
-    dt_copies = to_all("dp", n, dterm, t_send.at[0], t_recv.at[0])
+    grad_parts = three_parts(low_grad * factor, 0)
+    term_first = []
+    for h in range(HALVES):
+        dterm[h, 0] = add_parts(
+            jnp.dot(
+                grad_parts, tok_ref[:, pl.ds(h * half, half)], preferred_element_type=F32
+            ),
+            rank,
+        )
+        term_first.append(route_first(dterm, dt_sem, h))
     for s, i in partials[EARLY:LATE]:
         send_partial(s, i)
-
-    arrive(down_copies)
-    lbuf[1, 0] = dot_last(dbuf[from_owner], tok_ref[...])
+    if shared:
+        z_copies[0].wait_recv()
+        block = wx.at[0, beside]
+        last_y = remote(block, block, hop_sem.at[0, 2, 0], hop_sem.at[1, 2, 0], {"groups": 1 - y})
+        y_copies[1].wait_recv()
+        block = wx.at[1, across]
+        last_z = remote(block, block, hop_sem.at[0, 2, 1], hop_sem.at[1, 2, 1], {"dp": z_near})
+        share_copies += [last_y, last_z]
+
+    for copies in down_second:
+        arrive(copies)
+    down = [route_pick(dbuf, h, my_owner) for h in range(HALVES)]
+    lbuf[1, 0] = sum(
+        dot_last(down[h], tok_ref[:, pl.ds(h * half, half)]) for h in range(HALVES)
+    )
     li_copies = to_all("tensor", tn, lbuf.at[1], l_send.at[1], l_recv.at[1])
     for s, i in partials[LATE:]:
         send_partial(s, i)
+    term_second = [
+        route_second(dterm, tstage, dt_sem, h, term_first[h], near_user) for h in range(HALVES)
+    ]
     arrive(li_copies)
     uterm[0] = add_parts(
         jnp.dot(
@@ -260,33 +395,46 @@
     ut_copies = to_all("dp", n, uterm, t_send.at[1], t_recv.at[1])
 
     left = three_parts(jnp.transpose(adapter_scale * low_grad), 1)
+    whole_down = jnp.concatenate(down, axis=1)
     for i in range(chunks):
-        span = pl.ds(i * chunk, chunk)
-        down = dbuf[from_owner, :, span]
+        part = whole_down[:, i * chunk : (i + 1) * chunk]
         acc[i] = product(0, i) + jnp.dot(
-            left, jnp.concatenate([down, down, down], axis=0), preferred_element_type=F32
-        )
-    for i in range(chunks):
+            left, jnp.concatenate([part, part, part], axis=0), preferred_element_type=F32
+        )
+    for copies in term_second:
+        arrive(copies)
+    arrive(ut_copies)
+    for k in range(per):
+        here = jnp.where(kept == k, 1.0, 0.0).astype(F32)
+        for h in range(HALVES):
+            gdown_ref[k, :, pl.ds(h * half, half)] = route_pick(dterm, h, user) * here
+        gup_ref[k] = uterm[from_user] * here
+    if shared:
+        gx_other.wait_recv()
+        arrive([y_copies[0], z_copies[1], last_y, last_z])
+        per_chunk = 4 // shared
+        for i in range(shared):
+            total = acc[i]
+            for r in range(CORES):
+                rows = jnp.concatenate(
+                    [wx[r, q] for q in range(i * per_chunk, (i + 1) * per_chunk)], axis=0
+                )
+                total = total + dot_last(gx[r], rows)
+            out_ref[:, pl.ds(i * chunk, chunk)] = total.astype(BF16)
+    for i in range(shared, chunks):
         total = acc[i]
         for s in range(1, chips):
             p_copies[s, i].wait_recv()
             total = total + prec[s - 1, i]
         out_ref[:, pl.ds(i * chunk, chunk)] = total.astype(BF16)
 
-    arrive(dt_copies)
-    arrive(ut_copies)
-    for k in range(per):
-        mine = jnp.where(kept == k, 1.0, 0.0).astype(F32)
-        gdown_ref[k] = dterm[from_user] * mine
-        gup_ref[k] = uterm[from_user] * mine
-
     g_copy.wait_send()
     for group in (
         up_copies,
-        down_copies,
+        routed,
+        share_copies,
         lg_copies,
         li_copies,
-        dt_copies,
         ut_copies,
         w_copies.values(),
         p_copies.values(),
@@ -309,6 +457,7 @@
 
 
 def on_device(
+    groups,
     n,
     tn,
     entered_tokens,
@@ -326,10 +475,12 @@
     chips = tn // CORES
     chunk = min(512, feat)
     chunks = feat // chunk
+    shared = SHARED if chips == 2 and groups == 2 and n % 2 == 0 and chunks > SHARED else 0
+    quarter = max(shared * chunk // 4, 16)
     vmem = pl.BlockSpec(memory_space=pltpu.VMEM)
     dma = pltpu.SemaphoreType.DMA
     results = pl.pallas_call(
-        functools.partial(kernel, n, tn, chunk),
+        functools.partial(kernel, n, tn, chunk, shared),
         out_shape=(
             jax.ShapeDtypeStruct((tokens, feat), BF16),
             jax.ShapeDtypeStruct((per, rank, feat), F32),
@@ -348,11 +499,15 @@
             pltpu.VMEM((chips, feat, cols), BF16),
             pltpu.VMEM((chips, feat, cols), BF16),
             pltpu.VMEM((tokens, cols), BF16),
-            pltpu.VMEM((n, rank, feat), BF16),
+            pltpu.VMEM((HALVES, n, rank, feat // HALVES), BF16),
+            pltpu.VMEM((HALVES, rank, feat // HALVES), BF16),
             pltpu.VMEM((n, rank, cols), BF16),
             pltpu.VMEM((2, tn, rank, tokens), F32),
-            pltpu.VMEM((n, rank, feat), F32),
+            pltpu.VMEM((HALVES, n, rank, feat // HALVES), F32),
+            pltpu.VMEM((HALVES, rank, feat // HALVES), F32),
             pltpu.VMEM((n, rank, cols), F32),
+            pltpu.VMEM((CORES, 4, quarter, cols), BF16),
+            pltpu.VMEM((CORES, tokens, cols), BF16),
             pltpu.VMEM((chips - 1, chunks, tokens, chunk), F32),
             pltpu.VMEM((chips - 1, chunks, tokens, chunk), F32),
             pltpu.VMEM((chunks, tokens, chunk), F32),
@@ -368,6 +523,11 @@
             dma((2, n - 1)),
             dma((chips - 1, chunks)),
             dma((chips - 1, chunks)),
+            dma((2, HALVES, n)),
+            dma((2, HALVES, n)),
+            dma((2, CORES)),
+            dma((2, 3, CORES)),
+            dma((2, 2)),
         ],
         compiler_params=pltpu.CompilerParams(
             collective_id=0, has_side_effects=True, vmem_limit_bytes=VMEM_LIMIT
@@ -409,7 +569,7 @@
         P(("groups", "dp"), None, "tensor"),
         P(("groups", "dp"), None, "tensor"),
     )
-    body = functools.partial(on_device, mesh.shape["dp"], mesh.shape["tensor"])
+    body = functools.partial(on_device, mesh.shape["groups"], mesh.shape["dp"], mesh.shape["tensor"])
     return jax.shard_map(
         body, mesh=mesh, in_specs=in_specs, out_specs=out_specs, check_vma=False
     )

time: 37.2 us -> 33.3 us (0.90)
  Pallas kernels: 36.4 us -> 32.5 us
    pallas_call x1, Pallas kernels: 34.5 us -> 30.5 us  [on_device(): pl.pallas_call(functools.partial(kernel, n, tn, chunk, shared), out_shape...]
where the time goes in v4:
time: 33.3 us; the launch traced here: 33.1 us
  Pallas kernels  32.5 us (98%)
  between operations  0.64 us (2%)
    pallas_call x1, Pallas kernels, on_device(): pl.pallas_call(functools.partial(kernel, n, tn, chunk, shared), out_shape...  30.5 us
    pallas_call x1, Pallas kernels, on_device(): pl.pallas_call(write_out, out_shape=tuple((jax.ShapeDtypeStruct(r.shape,...  1.97 us

profile of v4, /device:TPU:0, one launch (start us, length us, event | category | flops | bytes accessed | tf_op | source)
XLA Modules:
  0.0 33.1 jit_solution(2821728052076765592)
XLA Ops:
  0.6 30.5 %shard_map.94 = (bf16[128,2048]{1,0:T(8,128)(2,1)}, f32[2,16,2048]{2,1,0:T(8,128)}, f32[2,16,256]{2,1,0:T(8,128)}) custom-call(s32[4]{0:T(128)} %seg_hbm.1, s32[8]{0:T(128)} %store_hbm.1, bf16[128,2048]{1,0:T(8,128)(2,1)} %tok_hbm.1, bf16[128,256]{1,0:T(8,128)(2,1)} %grad_hbm.1, bf16[8192,256]{1,0:T(8,128)(2,1)} %w_ref.1, bf16[2,16,2048]{2,1,0:T(8,128)(2,1)} %down_hbm.1, ...), custom_call_target="tpu_custom_call" | custom-call | flops 536870912 | bytes 4194304 | tf_op jit(solution)/shard_map/pallas_call | solution.py:482
  31.1 2.0 %shard_map.95 = (bf16[128,2048]{1,0:T(8,128)(2,1)}, f32[2,16,2048]{2,1,0:T(8,128)}, f32[2,16,256]{2,1,0:T(8,128)}) custom-call(bf16[128,2048]{1,0:T(8,128)(2,1)} %get-tuple-element.6.a, f32[2,16,2048]{2,1,0:T(8,128)} %get-tuple-element.7.b, f32[2,16,256]{2,1,0:T(8,128)} %get-tuple-element.8.c), custom_call_target="tpu_custom_call" | custom-call | tf_op jit(solution)/shard_map/pallas_call | solution.py:547

commit v5 on v4

--- a/solution.py
+++ b/solution.py
@@ -256,23 +256,19 @@
         mine = y * 2 + lax.rem(z, 2)
         across = (1 - y) * 2 + lax.rem(z, 2)
         beside = y * 2 + 1 - lax.rem(z, 2)
-        x_copies = []
-        for r in range(CORES):
+
+        def share_x(r):
             core = c if r == 0 else 1 - c
             start = ((1 - x) * CORES + core) * feat + mine * quarter
-            x_copies.append(
-                remote(
-                    w_ref.at[pl.ds(pl.multiple_of(start, quarter), quarter)],
-                    wx.at[r, mine],
-                    x_sem.at[0, r],
-                    x_sem.at[1, r],
-                    {"tensor": (1 - x) * CORES + core},
-                )
+            return remote(
+                w_ref.at[pl.ds(pl.multiple_of(start, quarter), quarter)],
+                wx.at[r, mine],
+                x_sem.at[0, r],
+                x_sem.at[1, r],
+                {"tensor": (1 - x) * CORES + core},
             )
-        gx_copy = remote(
-            grad_ref, gx.at[0], gx_sem.at[0, 0], gx_sem.at[1, 0], {"tensor": (1 - x) * CORES + c}
-        )
-        share_copies += x_copies + [gx_copy]
+
+        x_copies = [share_x(0)]
     g_copy = pltpu.make_async_remote_copy(
         src_ref=grad_ref,
         dst_ref=g_sib,
@@ -324,6 +320,12 @@
     arrive(up_copies)
     lbuf[0, 0] = dot_last(ubuf[from_owner], grad_ref[...])
     lg_copies = to_all("tensor", tn, lbuf.at[0], l_send.at[0], l_recv.at[0])
+    if shared:
+        x_copies.append(share_x(1))
+        gx_copy = remote(
+            grad_ref, gx.at[0], gx_sem.at[0, 0], gx_sem.at[1, 0], {"tensor": (1 - x) * CORES + c}
+        )
+        share_copies += x_copies + [gx_copy]
     g_copy.wait_recv()
     for s, i in partials[:EARLY]:
         send_partial(s, i)
@@ -443,15 +445,13 @@
             cp.wait_send()
 
 
-def write_out(a, b, c, a_out, b_out, c_out, a_held, b_held, c_held, sem):
-    rows = ((a, a_held, a_out), (b, b_held, b_out), (c, c_held, c_out))
-    loads = [pltpu.make_async_copy(r[0], r[1], sem.at[0, k]) for k, r in enumerate(rows)]
-    stores = [pltpu.make_async_copy(r[1], r[2], sem.at[1, k]) for k, r in enumerate(rows)]
-    for cp in loads:
+def write_out(a, b, c, a_out, b_out, c_out, sem):
+    stores = [
+        pltpu.make_async_copy(src, dst, sem.at[k])
+        for k, (src, dst) in enumerate(((a, a_out), (b, b_out), (c, c_out)))
+    ]
+    for cp in stores:
         cp.start()
-    for load, store in zip(loads, stores):
-        load.wait()
-        store.start()
     for cp in stores:
         cp.wait()
 
@@ -482,9 +482,9 @@
     results = pl.pallas_call(
         functools.partial(kernel, n, tn, chunk, shared),
         out_shape=(
-            jax.ShapeDtypeStruct((tokens, feat), BF16),
-            jax.ShapeDtypeStruct((per, rank, feat), F32),
-            jax.ShapeDtypeStruct((per, rank, cols), F32),
+            pltpu.VMEM((tokens, feat), BF16),
+            pltpu.VMEM((per, rank, feat), F32),
+            pltpu.VMEM((per, rank, cols), F32),
         ),
         in_specs=[pl.BlockSpec(memory_space=pltpu.HBM)] * 7,
         out_specs=(vmem, vmem, vmem),
@@ -549,8 +549,8 @@
         out_shape=tuple(jax.ShapeDtypeStruct(r.shape, r.dtype) for r in results),
         in_specs=[pl.BlockSpec(memory_space=pl.ANY)] * 3,
         out_specs=(pl.BlockSpec(memory_space=pl.ANY),) * 3,
-        scratch_shapes=[pltpu.VMEM(r.shape, r.dtype) for r in results] + [dma((2, 3))],
-        compiler_params=pltpu.CompilerParams(vmem_limit_bytes=VMEM_LIMIT),
+        scratch_shapes=[dma((3,))],
+        compiler_params=pltpu.CompilerParams(vmem_limit_bytes=4 * 1024 * 1024),
     )(*results)
 
 

time: 33.3 us -> 30.9 us (0.928)
  Pallas kernels: 32.5 us -> 30.1 us
    pallas_call x1, Pallas kernels: 30.5 us -> 29.2 us  [on_device(): pl.pallas_call(functools.partial(kernel, n, tn, chunk, shared), out_shape...]
    pallas_call x1, Pallas kernels: 1.97 us -> 0.91 us  [on_device(): pl.pallas_call(write_out, out_shape=tuple((jax.ShapeDtypeStruct(r.shape,...]
where the time goes in v5:
time: 30.9 us; the launch traced here: 30.7 us
  Pallas kernels  30.1 us (97%)
  between operations  0.64 us (2%)
    pallas_call x1, Pallas kernels, on_device(): pl.pallas_call(functools.partial(kernel, n, tn, chunk, shared), out_shape...  29.2 us
    pallas_call x1, Pallas kernels, on_device(): pl.pallas_call(write_out, out_shape=tuple((jax.ShapeDtypeStruct(r.shape,...  0.91 us

profile of v5, /device:TPU:0, one launch (start us, length us, event | category | flops | bytes accessed | tf_op | source)
XLA Modules:
  0.0 30.7 jit_solution(11658930613936591793)
XLA Ops:
  0.6 29.2 %shard_map.94 = (bf16[128,2048]{1,0:T(8,128)(2,1)S(1)}, f32[2,16,2048]{2,1,0:T(8,128)S(1)}, f32[2,16,256]{2,1,0:T(8,128)S(1)}) custom-call(s32[4]{0:T(128)} %seg_hbm.1, s32[8]{0:T(128)} %store_hbm.1, bf16[128,2048]{1,0:T(8,128)(2,1)} %tok_hbm.1, bf16[128,256]{1,0:T(8,128)(2,1)} %grad_hbm.1, bf16[8192,256]{1,0:T(8,128)(2,1)} %w_ref.1, ...), custom_call_target="tpu_custom_call" | custom-call | flops 536870912 | bytes 4194304 | tf_op jit(solution)/shard_map/pallas_call | solution.py:482
  29.8 0.9 %shard_map.95 = (bf16[128,2048]{1,0:T(8,128)(2,1)}, f32[2,16,2048]{2,1,0:T(8,128)}, f32[2,16,256]{2,1,0:T(8,128)}) custom-call(bf16[128,2048]{1,0:T(8,128)(2,1)S(1)} %get-tuple-element.6.a, f32[2,16,2048]{2,1,0:T(8,128)S(1)} %get-tuple-element.7.b, f32[2,16,256]{2,1,0:T(8,128)S(1)} %get-tuple-element.8.c), custom_call_target="tpu_custom_call" | custom-call | tf_op jit(solution)/shard_map/pallas_call | solution.py:547
